TPU v7x, 1024 devices: a whole 4x4x32 slice. The times are simulated.
1024 devices in a mesh: row: 16 (over x, y), depth: 64 (over z, core).
Axes of the slice: x: 4, y: 4, z: 32, core: 2. Of those that a mesh axis runs over, the one named last changes fastest.
Arguments:
- integrals: bfloat16 [45056, 40960], P('row', 'depth'), may hold values from -0.02734375 to 0.02734375
- amplitudes: bfloat16 [45056, 200], P(('row', 'depth')), may hold values from -6 to 6
Outputs:
- ladder: bfloat16 [40960, 200], P('depth')
All inputs are finite; a program needn't handle non-finite values.
Results may differ from a plain program's by a relative error of at most 0.001.
Values may be sent and summed in bfloat16 or wider, within the bound.
No kernel may reach another device: no remote copies, remote signals or barrier semaphores. Data moves between devices by JAX's collectives and lax.ppermute only.
A program may use at most 32 MiB of HBM per device.

v0:
```python
import jax
import jax.numpy as jnp
from jax import lax
from jax.sharding import PartitionSpec as P


def shards(integrals, amplitudes):
    partial_sum = lax.dot_general(
        integrals,
        lax.all_gather(amplitudes, "depth", axis=0, tiled=True),
        (((0,), (0,)), ((), ())),
        preferred_element_type=jnp.float32,
    )
    summed = lax.psum(partial_sum, "row")
    return summed.astype(jnp.bfloat16)


def solution(mesh):
    placed = (P("row", "depth"), P(("row", "depth"), None))
    return jax.shard_map(
        shards, mesh=mesh, in_specs=placed, out_specs=P("depth", None), check_vma=False
    )
```

profile of v0, /device:TPU:32, one launch (start us, length us, event | category | flops | bytes accessed | tf_op | source)
XLA Modules:
  0.0 245.6 jit_solution(18232111221665371747)
XLA Ops:
  6.5 0.0 all-gather.3.cloned.1.call-start
  6.5 0.7 all-gather.3.cloned.1.call-update
  7.3 145.5 %all-gather.3.cloned.1.call-done = bf16[64,44,200]{2,1,0:T(8,128)(2,1)} async-done(((bf16[1,44,200]{2,1,0:T(8,128)(2,1)}), bf16[64,44,200]{2,1,0:T(8,128)(2,1)}) %all-gather.3.cloned.1.call-update) | async-done | bytes 1126416 | tf_op jit(solution)/shard_map/all_gather | solution.py:10
  152.8 2.5 %reshape.1 = bf16[2816,200]{1,0:T(8,128)(2,1)S(1)} reshape(bf16[64,44,200]{2,1,0:T(8,128)(2,1)} %all-gather.3.cloned.1.call-done) | data formatting | bytes 2252800
  155.3 3.1 %fusion = f32[640,200]{0,1:T(8,128)S(1)} fusion(bf16[2816,640]{1,0:T(8,128)(2,1)} %param.2, bf16[2816,200]{1,0:T(8,128)(2,1)S(1)} %reshape.1), kind=kOutput, calls=%fused_computation | convolution fusion | flops 720896000 | bytes 5242880 | tf_op jit(solution)/shard_map/dot_general | solution.py:8
  158.4 80.4 %all-reduce.1 = bf16[640,200]{0,1:T(8,128)(2,1)} all-reduce(f32[640,200]{0,1:T(8,128)S(1)} %fusion), channel_id=1, replica_groups=mesh['row'=16,'depth'=64] {'row'}, use_global_device_ids=true, to_apply=%region_0.0 | all-reduce | flops 128000 | bytes 768000 | tf_op jit(solution)/shard_map/psum | solution.py:14
Async XLA Ops:
  6.5 146.2 %all-gather.3.cloned.1.call-start = ((), (), s32[]{:S(2)}) async-start(), calls=%async_computation | async-start | bytes 1597440 | tf_op jit(solution)/shard_map/all_gather | solution.py:10
Sparse Core Ops, SparseCore 0:
  10.1 142.6 all-gather.2
where the time goes:
time: 246 us
  waiting for transfers between devices  146 us (59%)
  blocking collectives  80.4 us (33%)
  between operations  13.4 us (5%)
  matrix products  3.11 us (1%)
  local copies, waits for them, and re-layouts  2.51 us (1%)
    all_gather x1, waiting for transfers between devices, shards(): lax.all_gather(amplitudes, 'depth', axis=0, tiled=True)  145 us
    psum x1, blocking collectives, shards(): summed = lax.psum(partial_sum, 'row')  80.4 us
  transfers between devices with their start and end apart: 1, of which 1 were waited for; matrix products, arithmetic and copies ran while one was open for 0% of the time, Pallas kernels for 0%

commit v1 on v0

v1 whole, which is shorter than its diff:
```python
import jax
import jax.numpy as jnp
from jax import lax
from jax.experimental import pallas as pl
from jax.experimental.pallas import tpu as pltpu
from jax.sharding import PartitionSpec as P

CUBE = 4
CORES = 2
LANES = 128
MIB = 1 << 20


def depth_groups(depth):
    cubes = depth // (CUBE * CORES)
    across = [
        [(b * CUBE + i) * CORES + c for b in range(cubes)]
        for i in range(CUBE)
        for c in range(CORES)
    ]
    inside = [
        [(b * CUBE + i) * CORES + c for i in range(CUBE)]
        for b in range(cubes)
        for c in range(CORES)
    ]
    return cubes, across, inside


def contract_kernel(core_ref, mine_ref, other_ref, integrals_hbm, out_ref, integrals, lines, turned, sem):
    chips, cubes, rows, ij = mine_ref.shape
    fetch = pltpu.make_async_copy(integrals_hbm, integrals, sem)
    fetch.start()
    first = core_ref[0] == 0
    for b in range(cubes):
        for i in range(chips):
            mine = mine_ref[i, b].astype(jnp.float32)
            other = other_ref[i, b].astype(jnp.float32)
            at = (b * chips + i) * CORES * rows
            lines[at : at + rows, :] = jnp.where(first, mine, other)
            lines[at + rows : at + 2 * rows, :] = jnp.where(first, other, mine)
    depth = lines.shape[0]
    for k in range(0, depth, 256):
        turned[:, k : k + 256] = lines[k : k + 256, :].T.astype(jnp.bfloat16)
    fetch.wait()
    for n in range(integrals.shape[1] // LANES):
        out_ref[n * ij : (n + 1) * ij, :] = jnp.dot(
            turned[...],
            integrals[:, n * LANES : (n + 1) * LANES],
            preferred_element_type=jnp.float32,
        )
    used = integrals.shape[1] // LANES * ij
    out_ref[used:, :] = jnp.zeros((out_ref.shape[0] - used, LANES), jnp.float32)


def contract(core, mine, other, integrals, lines_out):
    k, ab = integrals.shape
    ij = mine.shape[-1]
    vmem = pl.BlockSpec(memory_space=pltpu.VMEM)
    return pl.pallas_call(
        contract_kernel,
        out_shape=jax.ShapeDtypeStruct((lines_out, LANES), jnp.float32),
        in_specs=[
            pl.BlockSpec(memory_space=pltpu.SMEM),
            vmem,
            vmem,
            pl.BlockSpec(memory_space=pl.ANY),
        ],
        out_specs=vmem,
        scratch_shapes=[
            pltpu.VMEM((k, ab), jnp.bfloat16),
            pltpu.VMEM((k, ij), jnp.float32),
            pltpu.VMEM((ij, k), jnp.bfloat16),
            pltpu.SemaphoreType.DMA,
        ],
        compiler_params=pltpu.CompilerParams(vmem_limit_bytes=32 * MIB),
        cost_estimate=pl.CostEstimate(
            flops=2 * k * ab * ij, bytes_accessed=2 * k * (ab + ij), transcendentals=0
        ),
        name="contract",
    )(core, mine, other, integrals)


def total_kernel(terms_ref, out_ref):
    total = terms_ref[0]
    for r in range(1, terms_ref.shape[0]):
        total = total + terms_ref[r]
    total = total.astype(jnp.bfloat16)
    for r in range(out_ref.shape[0]):
        out_ref[r] = total


def totals(terms):
    vmem = pl.BlockSpec(memory_space=pltpu.VMEM)
    return pl.pallas_call(
        total_kernel,
        out_shape=jax.ShapeDtypeStruct(terms.shape, jnp.bfloat16),
        in_specs=[vmem],
        out_specs=vmem,
        name="totals",
    )(terms)


def order_kernel(lines_ref, out_ref):
    ij, ab = out_ref.shape
    for n in range(ab // LANES):
        out_ref[:, n * LANES : (n + 1) * LANES] = (
            lines_ref[n * ij : (n + 1) * ij, :]
            .astype(jnp.float32)
            .astype(jnp.bfloat16)
        )


def ordered(lines, ij, ab):
    vmem = pl.BlockSpec(memory_space=pltpu.VMEM)
    return pl.pallas_call(
        order_kernel,
        out_shape=jax.ShapeDtypeStruct((ij, ab), jnp.bfloat16),
        in_specs=[vmem],
        out_specs=vmem,
        name="ordered",
    )(lines)


def solution(mesh):
    rows, depth = mesh.shape["row"], mesh.shape["depth"]
    cubes, across, inside = depth_groups(depth)

    def shards(integrals, amplitudes):
        ij, ab = amplitudes.shape[1], integrals.shape[1]
        copies = jnp.broadcast_to(amplitudes[None], (cubes, *amplitudes.shape))
        mine = lax.all_to_all(copies, "depth", 0, 0, axis_index_groups=across)
        mine = lax.all_gather(mine, "depth", axis_index_groups=inside)
        other = lax.ppermute(mine, "depth", [(d, d ^ 1) for d in range(depth)])
        core = lax.rem(lax.axis_index("depth"), CORES).reshape(1)

        share = -(-ij * ab // (LANES * rows * 16)) * 16
        partial = contract(core, mine, other, integrals, rows * share)
        terms = lax.all_to_all(partial.reshape(rows, share, LANES), "row", 0, 0)
        whole = lax.all_to_all(totals(terms), "row", 0, 0)
        return ordered(whole.reshape(rows * share, LANES), ij, ab).T

    placed = (P("row", "depth"), P(("row", "depth"), None))
    return jax.shard_map(
        shards, mesh=mesh, in_specs=placed, out_specs=P("depth", None), check_vma=False
    )
```

time: 246 us -> 124 us (0.50)
  the two profiles are of different devices: /device:TPU:32 before, /device:TPU:8 now
where the time goes in v1:
time: 124 us
  blocking collectives  110 us (89%)
  Pallas kernels  6.41 us (5%)
  local copies, waits for them, and re-layouts  3.42 us (3%)
  starting transfers between devices  1.92 us (2%)
  waiting for transfers between devices  1.74 us (1%)
    all_to_all x1, blocking collectives, shards(): mine = lax.all_to_all(copies, 'depth', 0, 0, axis_index_groups=across)  59.5 us
    all_gather x1, blocking collectives, shards(): mine = lax.all_gather(mine, 'depth', axis_index_groups=inside)  20.7 us
    all_to_all x1, blocking collectives, shards(): terms = lax.all_to_all(partial.reshape(rows, share, LANES), 'row', 0, 0)  17.7 us
    all_to_all x1, blocking collectives, shards(): whole = lax.all_to_all(totals(terms), 'row', 0, 0)  12.5 us
    pallas_call x1, Pallas kernels, contract(): pl.pallas_call(contract_kernel, out_shape=jax.ShapeDtypeStruct((lines_out...  2.95 us
  transfers between devices with their start and end apart: 1, of which 1 were waited for; matrix products, arithmetic and copies ran while one was open for 0% of the time, Pallas kernels for 0%

profile of v1, /device:TPU:8, one launch (start us, length us, event | category | flops | bytes accessed | tf_op | source)
XLA Modules:
  0.0 124.0 jit_solution(5838494543657577935)
XLA Ops:
  0.0 0.8 broadcast_in_dim.2
  0.8 59.5 %all_to_all.15 = bf16[8,44,200]{2,1,0:T(8,128)(2,1)S(1)} all-to-all(bf16[8,44,200]{2,1,0:T(8,128)(2,1)S(1)} %broadcast_in_dim.2), channel_id=1, replica_groups={{0,8,16,24,32,40,48,56},{1,9,17,25,33,41,49,57},{2,10,18,26,34,42,50,58..., dimensions={0} | all-to-all | bytes 281600 | tf_op jit(solution)/shard_map/all_to_all | solution.py:131
  60.3 0.1 copy.6
  60.3 20.7 %all-gather = bf16[32,44,200]{2,0,1:T(8,128)(2,1)S(1)} all-gather(bf16[8,44,200]{2,0,1:T(8,128)(2,1)S(1)} %copy.6), channel_id=2, replica_groups={{0,2,4,6},{1,3,5,7},{8,10,12,14},{9,11,13,15},{16,18,20,22},{17,19,21,2..., dimensions={0}, use_global_device_ids=true | all-gather | bytes 704000 | tf_op jit(solution)/shard_map/all_gather | solution.py:132
  81.1 1.9 %collective-permute-start = (bf16[4,8,44,200]{3,1,2,0:T(8,128)(2,1)S(1)}, bf16[4,8,44,200]{3,1,2,0:T(8,128)(2,1)S(1)}, u32[]{:S(2)}, u32[]{:S(2)}) collective-permute-start(bf16[4,8,44,200]{3,1,2,0:T(8,128)(2,1)S(1)} %copy.8), channel_id=1, source_target_pairs={{0,1},{1,0},{2,3},{3,2},{4,5},{5,4},{6,7},{7,6},{8,9},{9,8},{10,11... | collective-permute-start | bytes 1689608 | tf_op jit(solution)/shard_map/ppermute | solution.py:133
  83.0 0.4 copy.7
  83.4 1.7 %collective-permute-done = bf16[4,8,44,200]{3,1,2,0:T(8,128)(2,1)S(1)} collective-permute-done((bf16[4,8,44,200]{3,1,2,0:T(8,128)(2,1)S(1)}, bf16[4,8,44,200]{3,1,2,0:T(8,128)(2,1)S(1)}, u32[]{:S(2)}, u32[]{:S(2)}) %collective-permute-start) | collective-permute-done | bytes 563232 | tf_op jit(solution)/shard_map/ppermute | solution.py:133
  85.2 0.1 copy.9.other_ref
  85.3 0.0 copy-start
  85.3 2.0 %copy-done = bf16[2816,640]{1,0:T(8,128)(2,1)S(1)} copy-done((bf16[2816,640]{1,0:T(8,128)(2,1)S(1)}, bf16[2816,640]{1,0:T(8,128)(2,1)}, u32[]{:S(2)}) %copy-start) | copy-done | bytes 3604504
  87.3 3.0 %contract.1 = f32[1024,128]{1,0:T(8,128)S(1)} custom-call(s32[1]{0:T(128)} %bitcast.core_ref, bf16[4,8,44,200]{3,2,1,0:T(8,128)(2,1)S(1)} %bitcast.6, bf16[4,8,44,200]{3,2,1,0:T(8,128)(2,1)S(1)} %copy.9.other_ref, bf16[2816,640]{1,0:T(8,128)(2,1)S(1)} %copy-done), custom_call_target="tpu_custom_call" | custom-call | flops 720896000 | bytes 4730880 | tf_op jit(solution)/shard_map/contract/pallas_call | solution.py:59
  90.3 17.7 %all_to_all.16.terms_ref = f32[16,64,128]{2,1,0:T(8,128)} all-to-all(f32[16,64,128]{2,1,0:T(8,128)S(1)} %bitcast.7), channel_id=1, replica_groups=mesh['row'=16,'depth'=64] {'row'}, dimensions={0} | all-to-all | bytes 1048576 | tf_op jit(solution)/shard_map/all_to_all | solution.py:138
  108.0 1.8 %totals.1 = bf16[16,64,128]{2,1,0:T(8,128)(2,1)} custom-call(f32[16,64,128]{2,1,0:T(8,128)} %all_to_all.16.terms_ref), custom_call_target="tpu_custom_call" | custom-call | tf_op jit(solution)/shard_map/totals/pallas_call | solution.py:94
  109.8 12.5 %all_to_all.17 = bf16[16,64,128]{2,1,0:T(8,128)(2,1)} all-to-all(bf16[16,64,128]{2,1,0:T(8,128)(2,1)} %totals.1), channel_id=1, replica_groups=mesh['row'=16,'depth'=64] {'row'}, dimensions={0} | all-to-all | bytes 524288 | tf_op jit(solution)/shard_map/all_to_all | solution.py:139
  122.3 1.7 %ordered.1 = bf16[200,640]{1,0:T(8,128)(2,1)} custom-call(bf16[1024,128]{1,0:T(8,128)(2,1)} %bitcast.9), custom_call_target="tpu_custom_call" | custom-call | tf_op jit(solution)/shard_map/ordered/pallas_call | solution.py:115
  (1 shorter events, 0.0 us)
Async XLA Ops:
  81.1 4.1 %collective-permute-start = (bf16[4,8,44,200]{3,1,2,0:T(8,128)(2,1)S(1)}, bf16[4,8,44,200]{3,1,2,0:T(8,128)(2,1)S(1)}, u32[]{:S(2)}, u32[]{:S(2)}) collective-permute-start(bf16[4,8,44,200]{3,1,2,0:T(8,128)(2,1)S(1)} %copy.8), channel_id=1, source_target_pairs={{0,1},{1,0},{2,3},{3,2},{4,5},{5,4},{6,7},{7,6},{8,9},{9,8},{10,11... | collective-permute-start | bytes 1689608 | tf_op jit(solution)/shard_map/ppermute | solution.py:133
  85.3 2.0 %copy-start = (bf16[2816,640]{1,0:T(8,128)(2,1)S(1)}, bf16[2816,640]{1,0:T(8,128)(2,1)}, u32[]{:S(2)}) copy-start(bf16[2816,640]{1,0:T(8,128)(2,1)} %integrals_hbm.1) | copy-start | bytes 10813444

commit v2 on v1

--- a/solution.py
+++ b/solution.py
@@ -13,31 +13,57 @@
 
 def depth_groups(depth):
     cubes = depth // (CUBE * CORES)
-    across = [
-        [(b * CUBE + i) * CORES + c for b in range(cubes)]
-        for i in range(CUBE)
-        for c in range(CORES)
-    ]
     inside = [
         [(b * CUBE + i) * CORES + c for i in range(CUBE)]
         for b in range(cubes)
         for c in range(CORES)
     ]
-    return cubes, across, inside
+    chips = [[d, d + 1] for d in range(0, depth, CORES)]
+    return cubes, inside, chips
 
 
-def contract_kernel(core_ref, mine_ref, other_ref, integrals_hbm, out_ref, integrals, lines, turned, sem):
+def hop(depth, cubes):
+    step = cubes * CUBE * CORES
+    return [(d, (d + step * (1 - 2 * (d % CORES))) % depth) for d in range(depth)]
+
+
+def spread(amplitudes, depth):
+    cubes, _, chips = depth_groups(depth)
+    pair = lax.all_gather(amplitudes, "depth", axis_index_groups=chips)
+    opposite = lax.ppermute(amplitudes, "depth", hop(depth, cubes // 2))
+    pairs = [
+        lax.ppermute(pair, "depth", hop(depth, k))
+        for k in range(cubes // 2 - 1, 0, -1)
+    ]
+    return jnp.concatenate([amplitudes[None], opposite[None], *pairs], axis=0)
+
+
+def contract_kernel(
+    place_ref, mine_ref, other_ref, integrals_hbm, out_ref, integrals, lines, turned, sem
+):
     chips, cubes, rows, ij = mine_ref.shape
     fetch = pltpu.make_async_copy(integrals_hbm, integrals, sem)
     fetch.start()
-    first = core_ref[0] == 0
-    for b in range(cubes):
-        for i in range(chips):
-            mine = mine_ref[i, b].astype(jnp.float32)
-            other = other_ref[i, b].astype(jnp.float32)
-            at = (b * chips + i) * CORES * rows
-            lines[at : at + rows, :] = jnp.where(first, mine, other)
-            lines[at + rows : at + 2 * rows, :] = jnp.where(first, other, mine)
+    cube, core = place_ref[0], place_ref[1]
+    first = core == 0
+    up = 1 - 2 * core
+
+    def put(b, i, upper, lower):
+        at = pl.multiple_of((b * chips + i) * (CORES * rows), 8)
+        lines[pl.ds(at, CORES * rows), :] = jnp.concatenate([upper, lower], axis=0)
+
+    def load(ref, i, j):
+        return ref[i, j].astype(jnp.float32)
+
+    for i in range(chips):
+        for j, away in ((0, 0), (1, cubes // 2)):
+            mine, other = load(mine_ref, i, j), load(other_ref, i, j)
+            upper, lower = jnp.where(first, mine, other), jnp.where(first, other, mine)
+            put(lax.rem(cube + away, cubes), i, upper, lower)
+        for j, k in enumerate(range(cubes // 2 - 1, 0, -1)):
+            for ref, sign in ((mine_ref, -up), (other_ref, up)):
+                b = lax.rem(cube + sign * k + cubes, cubes)
+                put(b, i, load(ref, i, 2 + 2 * j), load(ref, i, 3 + 2 * j))
     depth = lines.shape[0]
     for k in range(0, depth, 256):
         turned[:, k : k + 256] = lines[k : k + 256, :].T.astype(jnp.bfloat16)
@@ -52,7 +78,7 @@
     out_ref[used:, :] = jnp.zeros((out_ref.shape[0] - used, LANES), jnp.float32)
 
 
-def contract(core, mine, other, integrals, lines_out):
+def contract(place, mine, other, integrals, lines_out):
     k, ab = integrals.shape
     ij = mine.shape[-1]
     vmem = pl.BlockSpec(memory_space=pltpu.VMEM)
@@ -63,7 +89,7 @@
             pl.BlockSpec(memory_space=pltpu.SMEM),
             vmem,
             vmem,
-            pl.BlockSpec(memory_space=pl.ANY),
+            pl.BlockSpec(memory_space=pltpu.HBM),
         ],
         out_specs=vmem,
         scratch_shapes=[
@@ -77,7 +103,7 @@
             flops=2 * k * ab * ij, bytes_accessed=2 * k * (ab + ij), transcendentals=0
         ),
         name="contract",
-    )(core, mine, other, integrals)
+    )(place, mine, other, integrals)
 
 
 def total_kernel(terms_ref, out_ref):
@@ -123,18 +149,19 @@
 
 def solution(mesh):
     rows, depth = mesh.shape["row"], mesh.shape["depth"]
-    cubes, across, inside = depth_groups(depth)
+    _, inside, _ = depth_groups(depth)
 
     def shards(integrals, amplitudes):
         ij, ab = amplitudes.shape[1], integrals.shape[1]
-        copies = jnp.broadcast_to(amplitudes[None], (cubes, *amplitudes.shape))
-        mine = lax.all_to_all(copies, "depth", 0, 0, axis_index_groups=across)
-        mine = lax.all_gather(mine, "depth", axis_index_groups=inside)
+        mine = lax.all_gather(
+            spread(amplitudes, depth), "depth", axis_index_groups=inside
+        )
         other = lax.ppermute(mine, "depth", [(d, d ^ 1) for d in range(depth)])
-        core = lax.rem(lax.axis_index("depth"), CORES).reshape(1)
+        here = lax.axis_index("depth")
+        place = jnp.stack([here // (CUBE * CORES), lax.rem(here, CORES)])
 
         share = -(-ij * ab // (LANES * rows * 16)) * 16
-        partial = contract(core, mine, other, integrals, rows * share)
+        partial = contract(place, mine, other, integrals, rows * share)
         terms = lax.all_to_all(partial.reshape(rows, share, LANES), "row", 0, 0)
         whole = lax.all_to_all(totals(terms), "row", 0, 0)
         return ordered(whole.reshape(rows * share, LANES), ij, ab).T

time: 124 us -> 118 us (0.952)
  blocking collectives: 110 us -> 49.5 us
  starting transfers between devices: 1.92 us -> 44.3 us
  waiting for transfers between devices: 1.74 us -> 13.7 us
    all_to_all x1 -> x0, blocking collectives: 59.5 us -> none  [shards(): mine = lax.all_to_all(copies, 'depth', 0, 0, axis_index_groups=across)]
    ppermute x0 -> x4, starting transfers between devices: none -> 42.3 us  [the longest x1 29 us: spread(): opposite = lax.ppermute(amplitudes, 'depth', hop(depth, cubes // 2))]
    ppermute x0 -> x4, waiting for transfers between devices: none -> 12 us  [the longest x3 12 us: spread(): lax.ppermute(pair, 'depth', hop(depth, k))]
    all_gather x1 -> x2, blocking collectives: 20.7 us -> 19.2 us  [the longest x1 17.2 us: shards(): lax.all_gather(spread(amplitudes, depth), 'depth', axis_index_groups=inside)]
    unnamed x2 -> x6, local copies, waits for them, and re-layouts: 2.02 us -> 2.77 us
  transfers between devices with their start and end apart: 1 -> 5, of which waited for: 1 -> 2; matrix products, arithmetic and copies ran while one was open for 0% -> 1% of each run, Pallas kernels for 0% -> 0%
where the time goes in v2:
time: 118 us
  blocking collectives  49.5 us (42%)
  starting transfers between devices  44.3 us (38%)
  waiting for transfers between devices  13.7 us (12%)
  Pallas kernels  6.89 us (6%)
  local copies, waits for them, and re-layouts  3.43 us (3%)
    ppermute x1, starting transfers between devices, spread(): opposite = lax.ppermute(amplitudes, 'depth', hop(depth, cubes // 2))  29 us
    all_to_all x1, blocking collectives, shards(): terms = lax.all_to_all(partial.reshape(rows, share, LANES), 'row', 0, 0)  17.7 us
    all_gather x1, blocking collectives, shards(): lax.all_gather(spread(amplitudes, depth), 'depth', axis_index_groups=inside)  17.2 us
    ppermute x3, starting transfers between devices, spread(): lax.ppermute(pair, 'depth', hop(depth, k))  13.4 us
    all_to_all x1, blocking collectives, shards(): whole = lax.all_to_all(totals(terms), 'row', 0, 0)  12.5 us
    ppermute x3, waiting for transfers between devices, spread(): lax.ppermute(pair, 'depth', hop(depth, k))  12 us
    pallas_call x1, Pallas kernels, contract(): pl.pallas_call(contract_kernel, out_shape=jax.ShapeDtypeStruct((lines_out...  3.42 us
    unnamed x6, local copies, waits for them, and re-layouts  2.77 us
  transfers between devices with their start and end apart: 5, of which 2 were waited for; matrix products, arithmetic and copies ran while one was open for 1% of the time, Pallas kernels for 0%

profile of v2, /device:TPU:8, one launch (start us, length us, event | category | flops | bytes accessed | tf_op | source)
XLA Modules:
  0.0 117.9 jit_solution(11868475305625279070)
XLA Ops:
  0.0 29.0 %collective-permute-start = (bf16[44,200]{1,0:T(8,128)(2,1)}, bf16[44,200]{1,0:T(8,128)(2,1)S(1)}, u32[]{:S(2)}, u32[]{:S(2)}) collective-permute-start(bf16[44,200]{1,0:T(8,128)(2,1)} %param.3), channel_id=1, source_target_pairs={{0,32},{1,33},{2,34},{3,35},{4,36},{5,37},{6,38},{7,39},{8,40},{9,... | collective-permute-start | bytes 52808 | tf_op jit(solution)/shard_map/ppermute | solution.py:33
  29.0 2.1 %all-gather.2 = bf16[2,44,200]{2,1,0:T(8,128)(2,1)S(1)} all-gather(bf16[1,44,200]{2,1,0:T(8,128)(2,1)} %bitcast.15), channel_id=2, replica_groups={{0,1},{2,3},{4,5},{6,7},{8,9},{10,11},{12,13},{14,15},{16,17},{18,19},{..., dimensions={0}, use_global_device_ids=true | all-gather | bytes 52800 | tf_op jit(solution)/shard_map/all_gather | solution.py:32
  31.0 6.1 %collective-permute-start.2 = (bf16[2,44,200]{2,1,0:T(8,128)(2,1)S(1)}, bf16[2,44,200]{2,1,0:T(8,128)(2,1)S(1)}, u32[]{:S(2)}, u32[]{:S(2)}) collective-permute-start(bf16[2,44,200]{2,1,0:T(8,128)(2,1)S(1)} %all-gather.2), channel_id=1, source_target_pairs={{0,16},{1,49},{2,18},{3,51},{4,20},{5,53},{6,22},{7,55},{8,24},{9,... | collective-permute-start | bytes 105608 | tf_op jit(solution)/shard_map/ppermute | solution.py:35
  37.1 3.7 %collective-permute-start.1 = (bf16[2,44,200]{2,1,0:T(8,128)(2,1)S(1)}, bf16[2,44,200]{2,1,0:T(8,128)(2,1)S(1)}, u32[]{:S(2)}, u32[]{:S(2)}) collective-permute-start(bf16[2,44,200]{2,1,0:T(8,128)(2,1)S(1)} %all-gather.2), channel_id=1, source_target_pairs={{0,24},{1,41},{2,26},{3,43},{4,28},{5,45},{6,30},{7,47},{8,32},{9,... | collective-permute-start | bytes 105608 | tf_op jit(solution)/shard_map/ppermute | solution.py:35
  40.9 3.5 %collective-permute-start.3 = (bf16[2,44,200]{2,1,0:T(8,128)(2,1)S(1)}, bf16[2,44,200]{2,1,0:T(8,128)(2,1)S(1)}, u32[]{:S(2)}, u32[]{:S(2)}) collective-permute-start(bf16[2,44,200]{2,1,0:T(8,128)(2,1)S(1)} %all-gather.2), channel_id=1, source_target_pairs={{0,8},{1,57},{2,10},{3,59},{4,12},{5,61},{6,14},{7,63},{8,16},{9,1... | collective-permute-start | bytes 105608 | tf_op jit(solution)/shard_map/ppermute | solution.py:35
  44.4 0.7 constant_dynamic-update-slice_fusion.3
  45.2 0.0 collective-permute-done
  45.2 12.0 %collective-permute-done.1 = bf16[2,44,200]{2,1,0:T(8,128)(2,1)S(1)} collective-permute-done((bf16[2,44,200]{2,1,0:T(8,128)(2,1)S(1)}, bf16[2,44,200]{2,1,0:T(8,128)(2,1)S(1)}, u32[]{:S(2)}, u32[]{:S(2)}) %collective-permute-start.1) | collective-permute-done | bytes 35232 | tf_op jit(solution)/shard_map/ppermute | solution.py:35
  57.2 0.0 collective-permute-done.2
  57.2 0.0 collective-permute-done.3
  57.2 0.1 copy.3
  57.3 17.2 %all-gather.1 = bf16[32,44,200]{2,0,1:T(8,128)(2,1)S(1)} all-gather(bf16[8,44,200]{2,0,1:T(8,128)(2,1)S(1)} %copy.3), channel_id=3, replica_groups={{0,2,4,6},{1,3,5,7},{8,10,12,14},{9,11,13,15},{16,18,20,22},{17,19,21,2..., dimensions={0}, use_global_device_ids=true | all-gather | bytes 704000 | tf_op jit(solution)/shard_map/all_gather | solution.py:156
  74.5 1.9 %collective-permute-start.4 = (bf16[4,8,44,200]{3,1,2,0:T(8,128)(2,1)S(1)}, bf16[4,8,44,200]{3,1,2,0:T(8,128)(2,1)S(1)}, u32[]{:S(2)}, u32[]{:S(2)}) collective-permute-start(bf16[4,8,44,200]{3,1,2,0:T(8,128)(2,1)S(1)} %copy.5), channel_id=1, source_target_pairs={{0,1},{1,0},{2,3},{3,2},{4,5},{5,4},{6,7},{7,6},{8,9},{9,8},{10,11... | collective-permute-start | bytes 1689608 | tf_op jit(solution)/shard_map/ppermute | solution.py:159
  76.5 0.1 pad_add_fusion.place_ref
  76.5 0.4 copy.4
  77.0 1.7 %collective-permute-done.4 = bf16[4,8,44,200]{3,1,2,0:T(8,128)(2,1)S(1)} collective-permute-done((bf16[4,8,44,200]{3,1,2,0:T(8,128)(2,1)S(1)}, bf16[4,8,44,200]{3,1,2,0:T(8,128)(2,1)S(1)}, u32[]{:S(2)}, u32[]{:S(2)}) %collective-permute-start.4) | collective-permute-done | bytes 563232 | tf_op jit(solution)/shard_map/ppermute | solution.py:159
  78.6 0.1 copy.6.other_ref
  78.8 0.0 copy-start
  78.8 2.0 %copy-done = bf16[2816,640]{1,0:T(8,128)(2,1)S(1)} copy-done((bf16[2816,640]{1,0:T(8,128)(2,1)S(1)}, bf16[2816,640]{1,0:T(8,128)(2,1)}, u32[]{:S(2)}) %copy-start) | copy-done | bytes 3604504
  80.8 3.4 %contract.1 = f32[1024,128]{1,0:T(8,128)S(1)} custom-call(s32[2]{0:T(128)S(1)} %pad_add_fusion.place_ref, bf16[4,8,44,200]{3,2,1,0:T(8,128)(2,1)S(1)} %bitcast.11, bf16[4,8,44,200]{3,2,1,0:T(8,128)(2,1)S(1)} %copy.6.other_ref, bf16[2816,640]{1,0:T(8,128)(2,1)S(1)} %copy-done), custom_call_target="tpu_custom_call" | custom-call | flops 720896000 | bytes 4730880 | tf_op jit(solution)/shard_map/contract/pallas_call | solution.py:85
  84.2 17.7 %all_to_all.10.terms_ref = f32[16,64,128]{2,1,0:T(8,128)} all-to-all(f32[16,64,128]{2,1,0:T(8,128)S(1)} %bitcast.12), channel_id=1, replica_groups=mesh['row'=16,'depth'=64] {'row'}, dimensions={0} | all-to-all | bytes 1048576 | tf_op jit(solution)/shard_map/all_to_all | solution.py:165
  101.9 1.8 %totals.1 = bf16[16,64,128]{2,1,0:T(8,128)(2,1)} custom-call(f32[16,64,128]{2,1,0:T(8,128)} %all_to_all.10.terms_ref), custom_call_target="tpu_custom_call" | custom-call | tf_op jit(solution)/shard_map/totals/pallas_call | solution.py:120
  103.7 12.5 %all_to_all.11 = bf16[16,64,128]{2,1,0:T(8,128)(2,1)} all-to-all(bf16[16,64,128]{2,1,0:T(8,128)(2,1)} %totals.1), channel_id=1, replica_groups=mesh['row'=16,'depth'=64] {'row'}, dimensions={0} | all-to-all | bytes 524288 | tf_op jit(solution)/shard_map/all_to_all | solution.py:166
  116.2 1.7 %ordered.1 = bf16[200,640]{1,0:T(8,128)(2,1)} custom-call(bf16[1024,128]{1,0:T(8,128)(2,1)} %bitcast.14), custom_call_target="tpu_custom_call" | custom-call | tf_op jit(solution)/shard_map/ordered/pallas_call | solution.py:141
  (5 shorter events, 0.1 us)
Async XLA Ops:
  0.0 45.2 %collective-permute-start = (bf16[44,200]{1,0:T(8,128)(2,1)}, bf16[44,200]{1,0:T(8,128)(2,1)S(1)}, u32[]{:S(2)}, u32[]{:S(2)}) collective-permute-start(bf16[44,200]{1,0:T(8,128)(2,1)} %param.3), channel_id=1, source_target_pairs={{0,32},{1,33},{2,34},{3,35},{4,36},{5,37},{6,38},{7,39},{8,40},{9,... | collective-permute-start | bytes 52808 | tf_op jit(solution)/shard_map/ppermute | solution.py:33
  31.0 26.2 %collective-permute-start.2 = (bf16[2,44,200]{2,1,0:T(8,128)(2,1)S(1)}, bf16[2,44,200]{2,1,0:T(8,128)(2,1)S(1)}, u32[]{:S(2)}, u32[]{:S(2)}) collective-permute-start(bf16[2,44,200]{2,1,0:T(8,128)(2,1)S(1)} %all-gather.2), channel_id=1, source_target_pairs={{0,16},{1,49},{2,18},{3,51},{4,20},{5,53},{6,22},{7,55},{8,24},{9,... | collective-permute-start | bytes 105608 | tf_op jit(solution)/shard_map/ppermute | solution.py:35
  37.1 20.0 %collective-permute-start.1 = (bf16[2,44,200]{2,1,0:T(8,128)(2,1)S(1)}, bf16[2,44,200]{2,1,0:T(8,128)(2,1)S(1)}, u32[]{:S(2)}, u32[]{:S(2)}) collective-permute-start(bf16[2,44,200]{2,1,0:T(8,128)(2,1)S(1)} %all-gather.2), channel_id=1, source_target_pairs={{0,24},{1,41},{2,26},{3,43},{4,28},{5,45},{6,30},{7,47},{8,32},{9,... | collective-permute-start | bytes 105608 | tf_op jit(solution)/shard_map/ppermute | solution.py:35
  40.9 16.3 %collective-permute-start.3 = (bf16[2,44,200]{2,1,0:T(8,128)(2,1)S(1)}, bf16[2,44,200]{2,1,0:T(8,128)(2,1)S(1)}, u32[]{:S(2)}, u32[]{:S(2)}) collective-permute-start(bf16[2,44,200]{2,1,0:T(8,128)(2,1)S(1)} %all-gather.2), channel_id=1, source_target_pairs={{0,8},{1,57},{2,10},{3,59},{4,12},{5,61},{6,14},{7,63},{8,16},{9,1... | collective-permute-start | bytes 105608 | tf_op jit(solution)/shard_map/ppermute | solution.py:35
  74.5 4.1 %collective-permute-start.4 = (bf16[4,8,44,200]{3,1,2,0:T(8,128)(2,1)S(1)}, bf16[4,8,44,200]{3,1,2,0:T(8,128)(2,1)S(1)}, u32[]{:S(2)}, u32[]{:S(2)}) collective-permute-start(bf16[4,8,44,200]{3,1,2,0:T(8,128)(2,1)S(1)} %copy.5), channel_id=1, source_target_pairs={{0,1},{1,0},{2,3},{3,2},{4,5},{5,4},{6,7},{7,6},{8,9},{9,8},{10,11... | collective-permute-start | bytes 1689608 | tf_op jit(solution)/shard_map/ppermute | solution.py:159
  78.8 2.0 %copy-start = (bf16[2816,640]{1,0:T(8,128)(2,1)S(1)}, bf16[2816,640]{1,0:T(8,128)(2,1)}, u32[]{:S(2)}) copy-start(bf16[2816,640]{1,0:T(8,128)(2,1)} %integrals_hbm.1) | copy-start | bytes 10813444

commit v3 on v2

--- a/solution.py
+++ b/solution.py
@@ -22,6 +22,11 @@
     return cubes, inside, chips
 
 
+def distances(cubes):
+    far = list(range(cubes // 2 - 1, 0, -1))
+    return far[1:2] + far[:1] + far[2:]
+
+
 def hop(depth, cubes):
     step = cubes * CUBE * CORES
     return [(d, (d + step * (1 - 2 * (d % CORES))) % depth) for d in range(depth)]
@@ -33,7 +38,7 @@
     opposite = lax.ppermute(amplitudes, "depth", hop(depth, cubes // 2))
     pairs = [
         lax.ppermute(pair, "depth", hop(depth, k))
-        for k in range(cubes // 2 - 1, 0, -1)
+        for k in distances(cubes)
     ]
     return jnp.concatenate([amplitudes[None], opposite[None], *pairs], axis=0)
 
@@ -60,7 +65,7 @@
             mine, other = load(mine_ref, i, j), load(other_ref, i, j)
             upper, lower = jnp.where(first, mine, other), jnp.where(first, other, mine)
             put(lax.rem(cube + away, cubes), i, upper, lower)
-        for j, k in enumerate(range(cubes // 2 - 1, 0, -1)):
+        for j, k in enumerate(distances(cubes)):
             for ref, sign in ((mine_ref, -up), (other_ref, up)):
                 b = lax.rem(cube + sign * k + cubes, cubes)
                 put(b, i, load(ref, i, 2 + 2 * j), load(ref, i, 3 + 2 * j))
@@ -103,7 +108,7 @@
             flops=2 * k * ab * ij, bytes_accessed=2 * k * (ab + ij), transcendentals=0
         ),
         name="contract",
-    )(place, mine, other, integrals)
+    )(place, mine, other, pltpu.with_memory_space_constraint(integrals, pltpu.HBM))
 
 
 def total_kernel(terms_ref, out_ref):
@@ -122,6 +127,7 @@
         out_shape=jax.ShapeDtypeStruct(terms.shape, jnp.bfloat16),
         in_specs=[vmem],
         out_specs=vmem,
+        compiler_params=pltpu.CompilerParams(vmem_limit_bytes=4 * MIB),
         name="totals",
     )(terms)
 
@@ -143,6 +149,7 @@
         out_shape=jax.ShapeDtypeStruct((ij, ab), jnp.bfloat16),
         in_specs=[vmem],
         out_specs=vmem,
+        compiler_params=pltpu.CompilerParams(vmem_limit_bytes=4 * MIB),
         name="ordered",
     )(lines)
 

time: 118 us -> 115 us (0.975)
  local copies, waits for them, and re-layouts: 3.43 us -> 1.41 us
  Pallas kernels: 6.89 us -> 5.27 us
  blocking collectives: 49.5 us -> 50.8 us
    all_gather x1, blocking collectives: 17.2 us -> 19.6 us  [shards(): lax.all_gather(spread(amplitudes, depth), 'depth', axis_index_groups=inside)]
    unnamed x6 -> x4, local copies, waits for them, and re-layouts: 2.77 us -> 0.75 us
    pallas_call x1, Pallas kernels: 1.77 us -> 0.04 us  [totals(): pl.pallas_call(total_kernel, out_shape=jax.ShapeDtypeStruct(terms.shape,...]
  transfers between devices with their start and end apart: 5 -> 5, of which waited for: 2 -> 3; matrix products, arithmetic and copies ran while one was open for 1% -> 1% of each run, Pallas kernels for 0% -> 0%
where the time goes in v3:
time: 115 us
  blocking collectives  50.8 us (44%)
  starting transfers between devices  44.3 us (39%)
  waiting for transfers between devices  12.8 us (11%)
  Pallas kernels  5.27 us (5%)
  local copies, waits for them, and re-layouts  1.41 us (1%)
    ppermute x1, starting transfers between devices, spread(): opposite = lax.ppermute(amplitudes, 'depth', hop(depth, cubes // 2))  29 us
    all_gather x1, blocking collectives, shards(): lax.all_gather(spread(amplitudes, depth), 'depth', axis_index_groups=inside)  19.6 us
    all_to_all x1, blocking collectives, shards(): terms = lax.all_to_all(partial.reshape(rows, share, LANES), 'row', 0, 0)  17.6 us
    ppermute x3, starting transfers between devices, spread(): lax.ppermute(pair, 'depth', hop(depth, k))  13.4 us
    all_to_all x1, blocking collectives, shards(): whole = lax.all_to_all(totals(terms), 'row', 0, 0)  11.6 us
    ppermute x3, waiting for transfers between devices, spread(): lax.ppermute(pair, 'depth', hop(depth, k))  11.1 us
    pallas_call x1, Pallas kernels, contract(): pl.pallas_call(contract_kernel, out_shape=jax.ShapeDtypeStruct((lines_out...  4.49 us
  transfers between devices with their start and end apart: 5, of which 3 were waited for; matrix products, arithmetic and copies ran while one was open for 1% of the time, Pallas kernels for 0%

profile of v3, /device:TPU:8, one launch (start us, length us, event | category | flops | bytes accessed | tf_op | source)
XLA Modules:
  0.0 114.7 jit_solution(1283203380413399591)
XLA Ops:
  0.0 29.0 %collective-permute-start = (bf16[44,200]{1,0:T(8,128)(2,1)}, bf16[44,200]{1,0:T(8,128)(2,1)S(1)}, u32[]{:S(2)}, u32[]{:S(2)}) collective-permute-start(bf16[44,200]{1,0:T(8,128)(2,1)} %param.3), channel_id=1, source_target_pairs={{0,32},{1,33},{2,34},{3,35},{4,36},{5,37},{6,38},{7,39},{8,40},{9,... | collective-permute-start | bytes 52808 | tf_op jit(solution)/shard_map/ppermute | solution.py:38
  29.0 2.1 %all-gather.2 = bf16[2,44,200]{2,1,0:T(8,128)(2,1)S(1)} all-gather(bf16[1,44,200]{2,1,0:T(8,128)(2,1)} %bitcast.15), channel_id=2, replica_groups={{0,1},{2,3},{4,5},{6,7},{8,9},{10,11},{12,13},{14,15},{16,17},{18,19},{..., dimensions={0}, use_global_device_ids=true | all-gather | bytes 52800 | tf_op jit(solution)/shard_map/all_gather | solution.py:37
  31.0 7.9 %collective-permute-start.2 = (bf16[2,44,200]{2,1,0:T(8,128)(2,1)S(1)}, bf16[2,44,200]{2,1,0:T(8,128)(2,1)S(1)}, u32[]{:S(2)}, u32[]{:S(2)}) collective-permute-start(bf16[2,44,200]{2,1,0:T(8,128)(2,1)S(1)} %all-gather.2), channel_id=1, source_target_pairs={{0,24},{1,41},{2,26},{3,43},{4,28},{5,45},{6,30},{7,47},{8,32},{9,... | collective-permute-start | bytes 105608 | tf_op jit(solution)/shard_map/ppermute | solution.py:40
  38.9 1.9 %collective-permute-start.1 = (bf16[2,44,200]{2,1,0:T(8,128)(2,1)S(1)}, bf16[2,44,200]{2,1,0:T(8,128)(2,1)S(1)}, u32[]{:S(2)}, u32[]{:S(2)}) collective-permute-start(bf16[2,44,200]{2,1,0:T(8,128)(2,1)S(1)} %all-gather.2), channel_id=1, source_target_pairs={{0,16},{1,49},{2,18},{3,51},{4,20},{5,53},{6,22},{7,55},{8,24},{9,... | collective-permute-start | bytes 105608 | tf_op jit(solution)/shard_map/ppermute | solution.py:40
  40.9 3.5 %collective-permute-start.3 = (bf16[2,44,200]{2,1,0:T(8,128)(2,1)S(1)}, bf16[2,44,200]{2,1,0:T(8,128)(2,1)S(1)}, u32[]{:S(2)}, u32[]{:S(2)}) collective-permute-start(bf16[2,44,200]{2,1,0:T(8,128)(2,1)S(1)} %all-gather.2), channel_id=1, source_target_pairs={{0,8},{1,57},{2,10},{3,59},{4,12},{5,61},{6,14},{7,63},{8,16},{9,1... | collective-permute-start | bytes 105608 | tf_op jit(solution)/shard_map/ppermute | solution.py:40
  44.4 0.7 constant_dynamic-update-slice_fusion.3
  45.2 0.0 collective-permute-done
  45.2 9.5 %collective-permute-done.1 = bf16[2,44,200]{2,1,0:T(8,128)(2,1)S(1)} collective-permute-done((bf16[2,44,200]{2,1,0:T(8,128)(2,1)S(1)}, bf16[2,44,200]{2,1,0:T(8,128)(2,1)S(1)}, u32[]{:S(2)}, u32[]{:S(2)}) %collective-permute-start.1) | collective-permute-done | bytes 35232 | tf_op jit(solution)/shard_map/ppermute | solution.py:40
  54.7 0.0 collective-permute-done.2
  54.7 1.6 %collective-permute-done.3 = bf16[2,44,200]{2,1,0:T(8,128)(2,1)S(1)} collective-permute-done((bf16[2,44,200]{2,1,0:T(8,128)(2,1)S(1)}, bf16[2,44,200]{2,1,0:T(8,128)(2,1)S(1)}, u32[]{:S(2)}, u32[]{:S(2)}) %collective-permute-start.3) | collective-permute-done | bytes 35232 | tf_op jit(solution)/shard_map/ppermute | solution.py:40
  56.3 0.1 copy.3
  56.4 19.6 %all-gather.1 = bf16[32,44,200]{2,0,1:T(8,128)(2,1)S(1)} all-gather(bf16[8,44,200]{2,0,1:T(8,128)(2,1)S(1)} %copy.3), channel_id=3, replica_groups={{0,2,4,6},{1,3,5,7},{8,10,12,14},{9,11,13,15},{16,18,20,22},{17,19,21,2..., dimensions={0}, use_global_device_ids=true | all-gather | bytes 704000 | tf_op jit(solution)/shard_map/all_gather | solution.py:163
  76.0 1.9 %collective-permute-start.4 = (bf16[4,8,44,200]{3,1,2,0:T(8,128)(2,1)S(1)}, bf16[4,8,44,200]{3,1,2,0:T(8,128)(2,1)S(1)}, u32[]{:S(2)}, u32[]{:S(2)}) collective-permute-start(bf16[4,8,44,200]{3,1,2,0:T(8,128)(2,1)S(1)} %copy.5), channel_id=1, source_target_pairs={{0,1},{1,0},{2,3},{3,2},{4,5},{5,4},{6,7},{7,6},{8,9},{9,8},{10,11... | collective-permute-start | bytes 1689608 | tf_op jit(solution)/shard_map/ppermute | solution.py:166
  78.0 0.1 pad_add_fusion.place_ref
  78.0 0.4 copy.4
  78.4 1.7 %collective-permute-done.4 = bf16[4,8,44,200]{3,1,2,0:T(8,128)(2,1)S(1)} collective-permute-done((bf16[4,8,44,200]{3,1,2,0:T(8,128)(2,1)S(1)}, bf16[4,8,44,200]{3,1,2,0:T(8,128)(2,1)S(1)}, u32[]{:S(2)}, u32[]{:S(2)}) %collective-permute-start.4) | collective-permute-done | bytes 563232 | tf_op jit(solution)/shard_map/ppermute | solution.py:166
  80.1 0.1 copy.6.other_ref
  80.2 4.5 %contract.1 = f32[1024,128]{1,0:T(8,128)S(1)} custom-call(s32[2]{0:T(128)S(1)} %pad_add_fusion.place_ref, bf16[4,8,44,200]{3,2,1,0:T(8,128)(2,1)S(1)} %bitcast.11, bf16[4,8,44,200]{3,2,1,0:T(8,128)(2,1)S(1)} %copy.6.other_ref, bf16[2816,640]{1,0:T(8,128)(2,1)} %integrals_hbm.1), custom_call_target="tpu_custom_call" | custom-call | flops 720896000 | bytes 4730880 | tf_op jit(solution)/shard_map/contract/pallas_call | solution.py:90
  84.7 17.6 %all_to_all.10.terms_ref = f32[16,64,128]{2,1,0:T(8,128)S(1)} all-to-all(f32[16,64,128]{2,1,0:T(8,128)S(1)} %bitcast.12), channel_id=1, replica_groups=mesh['row'=16,'depth'=64] {'row'}, dimensions={0} | all-to-all | bytes 1048576 | tf_op jit(solution)/shard_map/all_to_all | solution.py:172
  102.4 11.6 %all_to_all.11 = bf16[16,64,128]{2,1,0:T(8,128)(2,1)S(1)} all-to-all(bf16[16,64,128]{2,1,0:T(8,128)(2,1)S(1)} %totals.1), channel_id=1, replica_groups=mesh['row'=16,'depth'=64] {'row'}, dimensions={0} | all-to-all | bytes 524288 | tf_op jit(solution)/shard_map/all_to_all | solution.py:173
  114.0 0.7 ordered.1
  (6 shorter events, 0.1 us)
Async XLA Ops:
  0.0 45.2 %collective-permute-start = (bf16[44,200]{1,0:T(8,128)(2,1)}, bf16[44,200]{1,0:T(8,128)(2,1)S(1)}, u32[]{:S(2)}, u32[]{:S(2)}) collective-permute-start(bf16[44,200]{1,0:T(8,128)(2,1)} %param.3), channel_id=1, source_target_pairs={{0,32},{1,33},{2,34},{3,35},{4,36},{5,37},{6,38},{7,39},{8,40},{9,... | collective-permute-start | bytes 52808 | tf_op jit(solution)/shard_map/ppermute | solution.py:38
  31.0 23.6 %collective-permute-start.2 = (bf16[2,44,200]{2,1,0:T(8,128)(2,1)S(1)}, bf16[2,44,200]{2,1,0:T(8,128)(2,1)S(1)}, u32[]{:S(2)}, u32[]{:S(2)}) collective-permute-start(bf16[2,44,200]{2,1,0:T(8,128)(2,1)S(1)} %all-gather.2), channel_id=1, source_target_pairs={{0,24},{1,41},{2,26},{3,43},{4,28},{5,45},{6,30},{7,47},{8,32},{9,... | collective-permute-start | bytes 105608 | tf_op jit(solution)/shard_map/ppermute | solution.py:40
  38.9 15.7 %collective-permute-start.1 = (bf16[2,44,200]{2,1,0:T(8,128)(2,1)S(1)}, bf16[2,44,200]{2,1,0:T(8,128)(2,1)S(1)}, u32[]{:S(2)}, u32[]{:S(2)}) collective-permute-start(bf16[2,44,200]{2,1,0:T(8,128)(2,1)S(1)} %all-gather.2), channel_id=1, source_target_pairs={{0,16},{1,49},{2,18},{3,51},{4,20},{5,53},{6,22},{7,55},{8,24},{9,... | collective-permute-start | bytes 105608 | tf_op jit(solution)/shard_map/ppermute | solution.py:40
  40.9 15.4 %collective-permute-start.3 = (bf16[2,44,200]{2,1,0:T(8,128)(2,1)S(1)}, bf16[2,44,200]{2,1,0:T(8,128)(2,1)S(1)}, u32[]{:S(2)}, u32[]{:S(2)}) collective-permute-start(bf16[2,44,200]{2,1,0:T(8,128)(2,1)S(1)} %all-gather.2), channel_id=1, source_target_pairs={{0,8},{1,57},{2,10},{3,59},{4,12},{5,61},{6,14},{7,63},{8,16},{9,1... | collective-permute-start | bytes 105608 | tf_op jit(solution)/shard_map/ppermute | solution.py:40
  76.0 4.1 %collective-permute-start.4 = (bf16[4,8,44,200]{3,1,2,0:T(8,128)(2,1)S(1)}, bf16[4,8,44,200]{3,1,2,0:T(8,128)(2,1)S(1)}, u32[]{:S(2)}, u32[]{:S(2)}) collective-permute-start(bf16[4,8,44,200]{3,1,2,0:T(8,128)(2,1)S(1)} %copy.5), channel_id=1, source_target_pairs={{0,1},{1,0},{2,3},{3,2},{4,5},{5,4},{6,7},{7,6},{8,9},{9,8},{10,11... | collective-permute-start | bytes 1689608 | tf_op jit(solution)/shard_map/ppermute | solution.py:166

commit v4 on v1

--- a/solution.py
+++ b/solution.py
@@ -5,39 +5,24 @@
 from jax.experimental.pallas import tpu as pltpu
 from jax.sharding import PartitionSpec as P
 
-CUBE = 4
 CORES = 2
 LANES = 128
 MIB = 1 << 20
 
 
-def depth_groups(depth):
-    cubes = depth // (CUBE * CORES)
-    across = [
-        [(b * CUBE + i) * CORES + c for b in range(cubes)]
-        for i in range(CUBE)
-        for c in range(CORES)
-    ]
-    inside = [
-        [(b * CUBE + i) * CORES + c for i in range(CUBE)]
-        for b in range(cubes)
-        for c in range(CORES)
-    ]
-    return cubes, across, inside
-
-
-def contract_kernel(core_ref, mine_ref, other_ref, integrals_hbm, out_ref, integrals, lines, turned, sem):
-    chips, cubes, rows, ij = mine_ref.shape
+def contract_kernel(
+    core_ref, mine_ref, other_ref, integrals_hbm, out_ref, integrals, lines, turned, sem
+):
+    chips, rows, ij = mine_ref.shape
     fetch = pltpu.make_async_copy(integrals_hbm, integrals, sem)
     fetch.start()
     first = core_ref[0] == 0
-    for b in range(cubes):
-        for i in range(chips):
-            mine = mine_ref[i, b].astype(jnp.float32)
-            other = other_ref[i, b].astype(jnp.float32)
-            at = (b * chips + i) * CORES * rows
-            lines[at : at + rows, :] = jnp.where(first, mine, other)
-            lines[at + rows : at + 2 * rows, :] = jnp.where(first, other, mine)
+    for z in range(chips):
+        mine = mine_ref[z].astype(jnp.float32)
+        other = other_ref[z].astype(jnp.float32)
+        upper, lower = jnp.where(first, mine, other), jnp.where(first, other, mine)
+        at = z * CORES * rows
+        lines[at : at + CORES * rows, :] = jnp.concatenate([upper, lower], axis=0)
     depth = lines.shape[0]
     for k in range(0, depth, 256):
         turned[:, k : k + 256] = lines[k : k + 256, :].T.astype(jnp.bfloat16)
@@ -63,7 +48,7 @@
             pl.BlockSpec(memory_space=pltpu.SMEM),
             vmem,
             vmem,
-            pl.BlockSpec(memory_space=pl.ANY),
+            pl.BlockSpec(memory_space=pltpu.HBM),
         ],
         out_specs=vmem,
         scratch_shapes=[
@@ -77,7 +62,7 @@
             flops=2 * k * ab * ij, bytes_accessed=2 * k * (ab + ij), transcendentals=0
         ),
         name="contract",
-    )(core, mine, other, integrals)
+    )(core, mine, other, pltpu.with_memory_space_constraint(integrals, pltpu.HBM))
 
 
 def total_kernel(terms_ref, out_ref):
@@ -96,6 +81,7 @@
         out_shape=jax.ShapeDtypeStruct(terms.shape, jnp.bfloat16),
         in_specs=[vmem],
         out_specs=vmem,
+        compiler_params=pltpu.CompilerParams(vmem_limit_bytes=4 * MIB),
         name="totals",
     )(terms)
 
@@ -117,20 +103,20 @@
         out_shape=jax.ShapeDtypeStruct((ij, ab), jnp.bfloat16),
         in_specs=[vmem],
         out_specs=vmem,
+        compiler_params=pltpu.CompilerParams(vmem_limit_bytes=4 * MIB),
         name="ordered",
     )(lines)
 
 
 def solution(mesh):
     rows, depth = mesh.shape["row"], mesh.shape["depth"]
-    cubes, across, inside = depth_groups(depth)
+    columns = [list(range(c, depth, CORES)) for c in range(CORES)]
+    swap = [(d, d ^ 1) for d in range(depth)]
 
     def shards(integrals, amplitudes):
         ij, ab = amplitudes.shape[1], integrals.shape[1]
-        copies = jnp.broadcast_to(amplitudes[None], (cubes, *amplitudes.shape))
-        mine = lax.all_to_all(copies, "depth", 0, 0, axis_index_groups=across)
-        mine = lax.all_gather(mine, "depth", axis_index_groups=inside)
-        other = lax.ppermute(mine, "depth", [(d, d ^ 1) for d in range(depth)])
+        mine = lax.all_gather(amplitudes, "depth", axis_index_groups=columns)
+        other = lax.ppermute(mine, "depth", swap)
         core = lax.rem(lax.axis_index("depth"), CORES).reshape(1)
 
         share = -(-ij * ab // (LANES * rows * 16)) * 16

time: 124 us -> 112 us (0.903)
  blocking collectives: 110 us -> 102 us
  local copies, waits for them, and re-layouts: 3.42 us -> 0.62 us
  Pallas kernels: 6.41 us -> 5.15 us
    all_to_all x1 -> x0, blocking collectives: 59.5 us -> none  [shards(): mine = lax.all_to_all(copies, 'depth', 0, 0, axis_index_groups=across)]
    all_gather x1, blocking collectives: 20.7 us -> 72.7 us  [shards(): mine = lax.all_gather(amplitudes, 'depth', axis_index_groups=columns)]
    unnamed x2 -> x0, local copies, waits for them, and re-layouts: 2.02 us -> none
    pallas_call x1, Pallas kernels: 1.77 us -> 0.04 us  [totals(): pl.pallas_call(total_kernel, out_shape=jax.ShapeDtypeStruct(terms.shape,...]
    pallas_call x1, Pallas kernels: 2.95 us -> 4.37 us  [contract(): pl.pallas_call(contract_kernel, out_shape=jax.ShapeDtypeStruct((lines_out...]
where the time goes in v4:
time: 112 us
  blocking collectives  102 us (91%)
  Pallas kernels  5.15 us (5%)
  waiting for transfers between devices  2.15 us (2%)
  starting transfers between devices  1.92 us (2%)
    all_gather x1, blocking collectives, shards(): mine = lax.all_gather(amplitudes, 'depth', axis_index_groups=columns)  72.7 us
    all_to_all x1, blocking collectives, shards(): terms = lax.all_to_all(partial.reshape(rows, share, LANES), 'row', 0, 0)  17.6 us
    all_to_all x1, blocking collectives, shards(): whole = lax.all_to_all(totals(terms), 'row', 0, 0)  11.6 us
    pallas_call x1, Pallas kernels, contract(): pl.pallas_call(contract_kernel, out_shape=jax.ShapeDtypeStruct((lines_out...  4.37 us
  transfers between devices with their start and end apart: 1, of which 1 were waited for; matrix products, arithmetic and copies ran while one was open for 0% of the time, Pallas kernels for 0%

profile of v4, /device:TPU:8, one launch (start us, length us, event | category | flops | bytes accessed | tf_op | source)
XLA Modules:
  0.0 111.7 jit_solution(14908268525482058670)
XLA Ops:
  0.0 72.7 %all-gather.1.mine_ref = bf16[32,44,200]{2,1,0:T(8,128)(2,1)S(1)} all-gather(bf16[1,44,200]{2,1,0:T(8,128)(2,1)} %bitcast.7), channel_id=2, replica_groups={{0,2,4,6,8,10,12,14,16,18,20,22,24,26,28,30,32,34,36,38,40,42,44,46,48,..., dimensions={0}, use_global_device_ids=true | all-gather | bytes 580800 | tf_op jit(solution)/shard_map/all_gather | solution.py:118
  72.7 0.2 copy.3
  72.9 1.9 %collective-permute-start = (bf16[32,44,200]{2,0,1:T(8,128)(2,1)S(1)}, bf16[32,44,200]{2,0,1:T(8,128)(2,1)S(1)}, u32[]{:S(2)}, u32[]{:S(2)}) collective-permute-start(bf16[32,44,200]{2,0,1:T(8,128)(2,1)S(1)} %copy.3), channel_id=1, source_target_pairs={{0,1},{1,0},{2,3},{3,2},{4,5},{5,4},{6,7},{7,6},{8,9},{9,8},{10,11... | collective-permute-start | bytes 1689608 | tf_op jit(solution)/shard_map/ppermute | solution.py:119
  74.8 2.2 %collective-permute-done = bf16[32,44,200]{2,0,1:T(8,128)(2,1)S(1)} collective-permute-done((bf16[32,44,200]{2,0,1:T(8,128)(2,1)S(1)}, bf16[32,44,200]{2,0,1:T(8,128)(2,1)S(1)}, u32[]{:S(2)}, u32[]{:S(2)}) %collective-permute-start) | collective-permute-done | bytes 563232 | tf_op jit(solution)/shard_map/ppermute | solution.py:119
  77.0 0.4 copy.4.other_ref
  77.4 4.4 %contract.1 = f32[1024,128]{1,0:T(8,128)S(1)} custom-call(s32[1]{0:T(128)} %bitcast.core_ref, bf16[32,44,200]{2,1,0:T(8,128)(2,1)S(1)} %all-gather.1.mine_ref, bf16[32,44,200]{2,1,0:T(8,128)(2,1)S(1)} %copy.4.other_ref, bf16[2816,640]{1,0:T(8,128)(2,1)} %integrals_hbm.1), custom_call_target="tpu_custom_call" | custom-call | flops 720896000 | bytes 4730880 | tf_op jit(solution)/shard_map/contract/pallas_call | solution.py:44
  81.7 17.6 %all_to_all.10.terms_ref = f32[16,64,128]{2,1,0:T(8,128)S(1)} all-to-all(f32[16,64,128]{2,1,0:T(8,128)S(1)} %bitcast.5), channel_id=1, replica_groups=mesh['row'=16,'depth'=64] {'row'}, dimensions={0} | all-to-all | bytes 1048576 | tf_op jit(solution)/shard_map/all_to_all | solution.py:124
  99.4 11.6 %all_to_all.11 = bf16[16,64,128]{2,1,0:T(8,128)(2,1)S(1)} all-to-all(bf16[16,64,128]{2,1,0:T(8,128)(2,1)S(1)} %totals.1), channel_id=1, replica_groups=mesh['row'=16,'depth'=64] {'row'}, dimensions={0} | all-to-all | bytes 524288 | tf_op jit(solution)/shard_map/all_to_all | solution.py:125
  111.0 0.7 ordered.1
  (1 shorter events, 0.0 us)
Async XLA Ops:
  72.9 4.1 %collective-permute-start = (bf16[32,44,200]{2,0,1:T(8,128)(2,1)S(1)}, bf16[32,44,200]{2,0,1:T(8,128)(2,1)S(1)}, u32[]{:S(2)}, u32[]{:S(2)}) collective-permute-start(bf16[32,44,200]{2,0,1:T(8,128)(2,1)S(1)} %copy.3), channel_id=1, source_target_pairs={{0,1},{1,0},{2,3},{3,2},{4,5},{5,4},{6,7},{7,6},{8,9},{9,8},{10,11... | collective-permute-start | bytes 1689608 | tf_op jit(solution)/shard_map/ppermute | solution.py:119

commit v5 on v4

--- a/solution.py
+++ b/solution.py
@@ -11,15 +11,16 @@
 
 
 def contract_kernel(
-    core_ref, mine_ref, other_ref, integrals_hbm, out_ref, integrals, lines, turned, sem
+    ring_ref, mine_ref, other_ref, integrals_hbm, out_ref, integrals, lines, turned, sem
 ):
     chips, rows, ij = mine_ref.shape
     fetch = pltpu.make_async_copy(integrals_hbm, integrals, sem)
     fetch.start()
-    first = core_ref[0] == 0
+    even = ring_ref[0] == 0
     for z in range(chips):
         mine = mine_ref[z].astype(jnp.float32)
         other = other_ref[z].astype(jnp.float32)
+        first = even if z % 2 == 0 else jnp.logical_not(even)
         upper, lower = jnp.where(first, mine, other), jnp.where(first, other, mine)
         at = z * CORES * rows
         lines[at : at + CORES * rows, :] = jnp.concatenate([upper, lower], axis=0)
@@ -27,17 +28,20 @@
     for k in range(0, depth, 256):
         turned[:, k : k + 256] = lines[k : k + 256, :].T.astype(jnp.bfloat16)
     fetch.wait()
-    for n in range(integrals.shape[1] // LANES):
-        out_ref[n * ij : (n + 1) * ij, :] = jnp.dot(
-            turned[...],
-            integrals[:, n * LANES : (n + 1) * LANES],
-            preferred_element_type=jnp.float32,
+    ab = integrals.shape[1]
+    for n in range(0, ab, 2 * LANES):
+        end = min(n + 2 * LANES, ab)
+        block = jnp.dot(
+            turned[...], integrals[:, n:end], preferred_element_type=jnp.float32
         )
-    used = integrals.shape[1] // LANES * ij
+        for m in range(n, end, LANES):
+            at = m // LANES * ij
+            out_ref[at : at + ij, :] = block[:, m - n : m - n + LANES]
+    used = ab // LANES * ij
     out_ref[used:, :] = jnp.zeros((out_ref.shape[0] - used, LANES), jnp.float32)
 
 
-def contract(core, mine, other, integrals, lines_out):
+def contract(ring, mine, other, integrals, lines_out):
     k, ab = integrals.shape
     ij = mine.shape[-1]
     vmem = pl.BlockSpec(memory_space=pltpu.VMEM)
@@ -62,7 +66,7 @@
             flops=2 * k * ab * ij, bytes_accessed=2 * k * (ab + ij), transcendentals=0
         ),
         name="contract",
-    )(core, mine, other, pltpu.with_memory_space_constraint(integrals, pltpu.HBM))
+    )(ring, mine, other, pltpu.with_memory_space_constraint(integrals, pltpu.HBM))
 
 
 def total_kernel(terms_ref, out_ref):
@@ -110,17 +114,21 @@
 
 def solution(mesh):
     rows, depth = mesh.shape["row"], mesh.shape["depth"]
-    columns = [list(range(c, depth, CORES)) for c in range(CORES)]
+    rings = [
+        [z * CORES + (q + z) % CORES for z in range(depth // CORES)]
+        for q in range(CORES)
+    ]
     swap = [(d, d ^ 1) for d in range(depth)]
 
     def shards(integrals, amplitudes):
         ij, ab = amplitudes.shape[1], integrals.shape[1]
-        mine = lax.all_gather(amplitudes, "depth", axis_index_groups=columns)
+        mine = lax.all_gather(amplitudes, "depth", axis_index_groups=rings)
         other = lax.ppermute(mine, "depth", swap)
-        core = lax.rem(lax.axis_index("depth"), CORES).reshape(1)
+        here = lax.axis_index("depth")
+        ring = lax.rem(here // CORES + here, CORES).reshape(1)
 
         share = -(-ij * ab // (LANES * rows * 16)) * 16
-        partial = contract(core, mine, other, integrals, rows * share)
+        partial = contract(ring, mine, other, integrals, rows * share)
         terms = lax.all_to_all(partial.reshape(rows, share, LANES), "row", 0, 0)
         whole = lax.all_to_all(totals(terms), "row", 0, 0)
         return ordered(whole.reshape(rows * share, LANES), ij, ab).T

time: 112 us -> 104 us (0.929)
  blocking collectives: 102 us -> 94.8 us
    all_gather x1, blocking collectives: 72.7 us -> 65.4 us  [shards(): mine = lax.all_gather(amplitudes, 'depth', axis_index_groups=rings)]
where the time goes in v5:
time: 104 us
  blocking collectives  94.8 us (91%)
  Pallas kernels  4.56 us (4%)
  starting transfers between devices  2.3 us (2%)
  waiting for transfers between devices  1.78 us (2%)
    all_gather x1, blocking collectives, shards(): mine = lax.all_gather(amplitudes, 'depth', axis_index_groups=rings)  65.4 us
    all_to_all x1, blocking collectives, shards(): terms = lax.all_to_all(partial.reshape(rows, share, LANES), 'row', 0, 0)  17.8 us
    all_to_all x1, blocking collectives, shards(): whole = lax.all_to_all(totals(terms), 'row', 0, 0)  11.6 us
    pallas_call x1, Pallas kernels, contract(): pl.pallas_call(contract_kernel, out_shape=jax.ShapeDtypeStruct((lines_out...  3.78 us
    ppermute x1, starting transfers between devices, shards(): other = lax.ppermute(mine, 'depth', swap)  2.3 us
  transfers between devices with their start and end apart: 1, of which 1 were waited for; matrix products, arithmetic and copies ran while one was open for 0% of the time, Pallas kernels for 0%

profile of v5, /device:TPU:8, one launch (start us, length us, event | category | flops | bytes accessed | tf_op | source)
XLA Modules:
  0.0 104.1 jit_solution(15012587035662606686)
XLA Ops:
  0.0 65.4 %all-gather.1.mine_ref = bf16[32,44,200]{2,1,0:T(8,128)(2,1)S(1)} all-gather(bf16[1,44,200]{2,1,0:T(8,128)(2,1)} %bitcast.7), channel_id=2, replica_groups={{0,3,4,7,8,11,12,15,16,19,20,23,24,27,28,31,32,35,36,39,40,43,44,47,48,..., dimensions={0}, use_global_device_ids=true | all-gather | bytes 580800 | tf_op jit(solution)/shard_map/all_gather | solution.py:125
  65.4 0.2 copy.3
  65.6 2.3 %collective-permute-start = (bf16[32,44,200]{2,0,1:T(8,128)(2,1)S(1)}, bf16[32,44,200]{2,0,1:T(8,128)(2,1)S(1)}, u32[]{:S(2)}, u32[]{:S(2)}) collective-permute-start(bf16[32,44,200]{2,0,1:T(8,128)(2,1)S(1)} %copy.3), channel_id=1, source_target_pairs={{0,1},{1,0},{2,3},{3,2},{4,5},{5,4},{6,7},{7,6},{8,9},{9,8},{10,11... | collective-permute-start | bytes 1689608 | tf_op jit(solution)/shard_map/ppermute | solution.py:126
  67.9 1.8 %collective-permute-done = bf16[32,44,200]{2,0,1:T(8,128)(2,1)S(1)} collective-permute-done((bf16[32,44,200]{2,0,1:T(8,128)(2,1)S(1)}, bf16[32,44,200]{2,0,1:T(8,128)(2,1)S(1)}, u32[]{:S(2)}, u32[]{:S(2)}) %collective-permute-start) | collective-permute-done | bytes 563232 | tf_op jit(solution)/shard_map/ppermute | solution.py:126
  69.7 0.4 copy.4.other_ref
  70.1 3.8 %contract.1 = f32[1024,128]{1,0:T(8,128)S(1)} custom-call(s32[1]{0:T(128)} %bitcast.ring_ref, bf16[32,44,200]{2,1,0:T(8,128)(2,1)S(1)} %all-gather.1.mine_ref, bf16[32,44,200]{2,1,0:T(8,128)(2,1)S(1)} %copy.4.other_ref, bf16[2816,640]{1,0:T(8,128)(2,1)} %integrals_hbm.1), custom_call_target="tpu_custom_call" | custom-call | flops 720896000 | bytes 4730880 | tf_op jit(solution)/shard_map/contract/pallas_call | solution.py:48
  73.9 17.8 %all_to_all.10.terms_ref = f32[16,64,128]{2,1,0:T(8,128)S(1)} all-to-all(f32[16,64,128]{2,1,0:T(8,128)S(1)} %bitcast.5), channel_id=1, replica_groups=mesh['row'=16,'depth'=64] {'row'}, dimensions={0} | all-to-all | bytes 1048576 | tf_op jit(solution)/shard_map/all_to_all | solution.py:132
  91.8 11.6 %all_to_all.11 = bf16[16,64,128]{2,1,0:T(8,128)(2,1)S(1)} all-to-all(bf16[16,64,128]{2,1,0:T(8,128)(2,1)S(1)} %totals.1), channel_id=1, replica_groups=mesh['row'=16,'depth'=64] {'row'}, dimensions={0} | all-to-all | bytes 524288 | tf_op jit(solution)/shard_map/all_to_all | solution.py:133
  103.4 0.7 ordered.1
  (1 shorter events, 0.0 us)
Async XLA Ops:
  65.6 4.1 %collective-permute-start = (bf16[32,44,200]{2,0,1:T(8,128)(2,1)S(1)}, bf16[32,44,200]{2,0,1:T(8,128)(2,1)S(1)}, u32[]{:S(2)}, u32[]{:S(2)}) collective-permute-start(bf16[32,44,200]{2,0,1:T(8,128)(2,1)S(1)} %copy.3), channel_id=1, source_target_pairs={{0,1},{1,0},{2,3},{3,2},{4,5},{5,4},{6,7},{7,6},{8,9},{9,8},{10,11... | collective-permute-start | bytes 1689608 | tf_op jit(solution)/shard_map/ppermute | solution.py:126

commit v6 on v5

--- a/solution.py
+++ b/solution.py
@@ -17,9 +17,10 @@
     fetch = pltpu.make_async_copy(integrals_hbm, integrals, sem)
     fetch.start()
     even = ring_ref[0] == 0
-    for z in range(chips):
-        mine = mine_ref[z].astype(jnp.float32)
-        other = other_ref[z].astype(jnp.float32)
+    for member in range(chips):
+        z = (member + chips // 2) % chips
+        mine = mine_ref[member].astype(jnp.float32)
+        other = other_ref[member].astype(jnp.float32)
         first = even if z % 2 == 0 else jnp.logical_not(even)
         upper, lower = jnp.where(first, mine, other), jnp.where(first, other, mine)
         at = z * CORES * rows
@@ -114,10 +115,9 @@
 
 def solution(mesh):
     rows, depth = mesh.shape["row"], mesh.shape["depth"]
-    rings = [
-        [z * CORES + (q + z) % CORES for z in range(depth // CORES)]
-        for q in range(CORES)
-    ]
+    chips = depth // CORES
+    order = [(member + chips // 2) % chips for member in range(chips)]
+    rings = [[z * CORES + (q + z) % CORES for z in order] for q in range(CORES)]
     swap = [(d, d ^ 1) for d in range(depth)]
 
     def shards(integrals, amplitudes):

time: 104 us -> 104 us (level)
  no operation moved by 1% of the time
where the time goes in v6:
time: 104 us
  blocking collectives  94.8 us (91%)
  Pallas kernels  4.56 us (4%)
  starting transfers between devices  2.3 us (2%)
  waiting for transfers between devices  1.78 us (2%)
    all_gather x1, blocking collectives, shards(): mine = lax.all_gather(amplitudes, 'depth', axis_index_groups=rings)  65.4 us
    all_to_all x1, blocking collectives, shards(): terms = lax.all_to_all(partial.reshape(rows, share, LANES), 'row', 0, 0)  17.9 us
    all_to_all x1, blocking collectives, shards(): whole = lax.all_to_all(totals(terms), 'row', 0, 0)  11.6 us
    pallas_call x1, Pallas kernels, contract(): pl.pallas_call(contract_kernel, out_shape=jax.ShapeDtypeStruct((lines_out...  3.78 us
    ppermute x1, starting transfers between devices, shards(): other = lax.ppermute(mine, 'depth', swap)  2.3 us
  transfers between devices with their start and end apart: 1, of which 1 were waited for; matrix products, arithmetic and copies ran while one was open for 0% of the time, Pallas kernels for 0%

profile of v6, /device:TPU:8, one launch (start us, length us, event | category | flops | bytes accessed | tf_op | source)
XLA Modules:
  0.0 104.1 jit_solution(17422723383605936608)
XLA Ops:
  0.0 65.4 %all-gather.1.mine_ref = bf16[32,44,200]{2,1,0:T(8,128)(2,1)S(1)} all-gather(bf16[1,44,200]{2,1,0:T(8,128)(2,1)} %bitcast.7), channel_id=2, replica_groups={{32,35,36,39,40,43,44,47,48,51,52,55,56,59,60,63,0,3,4,7,8,11,12,15,16,..., dimensions={0}, use_global_device_ids=true | all-gather | bytes 580800 | tf_op jit(solution)/shard_map/all_gather | solution.py:125
  65.4 0.2 copy.3
  65.6 2.3 %collective-permute-start = (bf16[32,44,200]{2,0,1:T(8,128)(2,1)S(1)}, bf16[32,44,200]{2,0,1:T(8,128)(2,1)S(1)}, u32[]{:S(2)}, u32[]{:S(2)}) collective-permute-start(bf16[32,44,200]{2,0,1:T(8,128)(2,1)S(1)} %copy.3), channel_id=1, source_target_pairs={{0,1},{1,0},{2,3},{3,2},{4,5},{5,4},{6,7},{7,6},{8,9},{9,8},{10,11... | collective-permute-start | bytes 1689608 | tf_op jit(solution)/shard_map/ppermute | solution.py:126
  67.9 1.8 %collective-permute-done = bf16[32,44,200]{2,0,1:T(8,128)(2,1)S(1)} collective-permute-done((bf16[32,44,200]{2,0,1:T(8,128)(2,1)S(1)}, bf16[32,44,200]{2,0,1:T(8,128)(2,1)S(1)}, u32[]{:S(2)}, u32[]{:S(2)}) %collective-permute-start) | collective-permute-done | bytes 563232 | tf_op jit(solution)/shard_map/ppermute | solution.py:126
  69.7 0.4 copy.4.other_ref
  70.1 3.8 %contract.1 = f32[1024,128]{1,0:T(8,128)S(1)} custom-call(s32[1]{0:T(128)} %bitcast.ring_ref, bf16[32,44,200]{2,1,0:T(8,128)(2,1)S(1)} %all-gather.1.mine_ref, bf16[32,44,200]{2,1,0:T(8,128)(2,1)S(1)} %copy.4.other_ref, bf16[2816,640]{1,0:T(8,128)(2,1)} %integrals_hbm.1), custom_call_target="tpu_custom_call" | custom-call | flops 720896000 | bytes 4730880 | tf_op jit(solution)/shard_map/contract/pallas_call | solution.py:49
  73.9 17.9 %all_to_all.10.terms_ref = f32[16,64,128]{2,1,0:T(8,128)S(1)} all-to-all(f32[16,64,128]{2,1,0:T(8,128)S(1)} %bitcast.5), channel_id=1, replica_groups=mesh['row'=16,'depth'=64] {'row'}, dimensions={0} | all-to-all | bytes 1048576 | tf_op jit(solution)/shard_map/all_to_all | solution.py:132
  91.8 11.6 %all_to_all.11 = bf16[16,64,128]{2,1,0:T(8,128)(2,1)S(1)} all-to-all(bf16[16,64,128]{2,1,0:T(8,128)(2,1)S(1)} %totals.1), channel_id=1, replica_groups=mesh['row'=16,'depth'=64] {'row'}, dimensions={0} | all-to-all | bytes 524288 | tf_op jit(solution)/shard_map/all_to_all | solution.py:133
  103.4 0.7 ordered.1
  (1 shorter events, 0.0 us)
Async XLA Ops:
  65.6 4.1 %collective-permute-start = (bf16[32,44,200]{2,0,1:T(8,128)(2,1)S(1)}, bf16[32,44,200]{2,0,1:T(8,128)(2,1)S(1)}, u32[]{:S(2)}, u32[]{:S(2)}) collective-permute-start(bf16[32,44,200]{2,0,1:T(8,128)(2,1)S(1)} %copy.3), channel_id=1, source_target_pairs={{0,1},{1,0},{2,3},{3,2},{4,5},{5,4},{6,7},{7,6},{8,9},{9,8},{10,11... | collective-permute-start | bytes 1689608 | tf_op jit(solution)/shard_map/ppermute | solution.py:126

commit v7 on v5

--- a/solution.py
+++ b/solution.py
@@ -16,6 +16,17 @@
     chips, rows, ij = mine_ref.shape
     fetch = pltpu.make_async_copy(integrals_hbm, integrals, sem)
     fetch.start()
+    members, share, _ = out_ref.shape
+
+    def put(line, values):
+        done = 0
+        while done < values.shape[0]:
+            owner, at = divmod(line + done, share)
+            size = min(share - at, values.shape[0] - done)
+            slot = members - 1 - owner
+            out_ref[slot, at : at + size, :] = values[done : done + size]
+            done += size
+
     even = ring_ref[0] == 0
     for z in range(chips):
         mine = mine_ref[z].astype(jnp.float32)
@@ -35,19 +46,19 @@
             turned[...], integrals[:, n:end], preferred_element_type=jnp.float32
         )
         for m in range(n, end, LANES):
-            at = m // LANES * ij
-            out_ref[at : at + ij, :] = block[:, m - n : m - n + LANES]
+            first_line = m // LANES * ij
+            put(first_line, block[:, m - n : m - n + LANES])
     used = ab // LANES * ij
-    out_ref[used:, :] = jnp.zeros((out_ref.shape[0] - used, LANES), jnp.float32)
+    put(used, jnp.zeros((members * share - used, LANES), jnp.float32))
 
 
-def contract(ring, mine, other, integrals, lines_out):
+def contract(ring, mine, other, integrals, rows, share):
     k, ab = integrals.shape
     ij = mine.shape[-1]
     vmem = pl.BlockSpec(memory_space=pltpu.VMEM)
     return pl.pallas_call(
         contract_kernel,
-        out_shape=jax.ShapeDtypeStruct((lines_out, LANES), jnp.float32),
+        out_shape=jax.ShapeDtypeStruct((rows, share, LANES), jnp.float32),
         in_specs=[
             pl.BlockSpec(memory_space=pltpu.SMEM),
             vmem,
@@ -119,6 +130,7 @@
         for q in range(CORES)
     ]
     swap = [(d, d ^ 1) for d in range(depth)]
+    turned = [list(range(rows))[::-1]]
 
     def shards(integrals, amplitudes):
         ij, ab = amplitudes.shape[1], integrals.shape[1]
@@ -128,8 +140,8 @@
         ring = lax.rem(here // CORES + here, CORES).reshape(1)
 
         share = -(-ij * ab // (LANES * rows * 16)) * 16
-        partial = contract(ring, mine, other, integrals, rows * share)
-        terms = lax.all_to_all(partial.reshape(rows, share, LANES), "row", 0, 0)
+        partial = contract(ring, mine, other, integrals, rows, share)
+        terms = lax.all_to_all(partial, "row", 0, 0, axis_index_groups=turned)
         whole = lax.all_to_all(totals(terms), "row", 0, 0)
         return ordered(whole.reshape(rows * share, LANES), ij, ab).T
 

time: 104 us -> 104 us (level)
    all_to_all x1, blocking collectives: 17.8 us -> 15.7 us  [shards(): terms = lax.all_to_all(partial, 'row', 0, 0, axis_index_groups=turned)]
    all_to_all x1, blocking collectives: 11.6 us -> 13.3 us  [shards(): whole = lax.all_to_all(totals(terms), 'row', 0, 0)]
where the time goes in v7:
time: 104 us
  blocking collectives  94.4 us (91%)
  Pallas kernels  4.56 us (4%)
  starting transfers between devices  2.3 us (2%)
  waiting for transfers between devices  1.78 us (2%)
    all_gather x1, blocking collectives, shards(): mine = lax.all_gather(amplitudes, 'depth', axis_index_groups=rings)  65.4 us
    all_to_all x1, blocking collectives, shards(): terms = lax.all_to_all(partial, 'row', 0, 0, axis_index_groups=turned)  15.7 us
    all_to_all x1, blocking collectives, shards(): whole = lax.all_to_all(totals(terms), 'row', 0, 0)  13.3 us
    pallas_call x1, Pallas kernels, contract(): pl.pallas_call(contract_kernel, out_shape=jax.ShapeDtypeStruct((rows, sha...  3.78 us
    ppermute x1, starting transfers between devices, shards(): other = lax.ppermute(mine, 'depth', swap)  2.3 us
  transfers between devices with their start and end apart: 1, of which 1 were waited for; matrix products, arithmetic and copies ran while one was open for 0% of the time, Pallas kernels for 0%

profile of v7, /device:TPU:8, one launch (start us, length us, event | category | flops | bytes accessed | tf_op | source)
XLA Modules:
  0.0 103.7 jit_solution(120518139746244782)
XLA Ops:
  0.0 65.4 %all-gather.1.mine_ref = bf16[32,44,200]{2,1,0:T(8,128)(2,1)S(1)} all-gather(bf16[1,44,200]{2,1,0:T(8,128)(2,1)} %bitcast.5), channel_id=2, replica_groups={{0,3,4,7,8,11,12,15,16,19,20,23,24,27,28,31,32,35,36,39,40,43,44,47,48,..., dimensions={0}, use_global_device_ids=true | all-gather | bytes 580800 | tf_op jit(solution)/shard_map/all_gather | solution.py:137
  65.4 0.2 copy.3
  65.6 2.3 %collective-permute-start = (bf16[32,44,200]{2,0,1:T(8,128)(2,1)S(1)}, bf16[32,44,200]{2,0,1:T(8,128)(2,1)S(1)}, u32[]{:S(2)}, u32[]{:S(2)}) collective-permute-start(bf16[32,44,200]{2,0,1:T(8,128)(2,1)S(1)} %copy.3), channel_id=1, source_target_pairs={{0,1},{1,0},{2,3},{3,2},{4,5},{5,4},{6,7},{7,6},{8,9},{9,8},{10,11... | collective-permute-start | bytes 1689608 | tf_op jit(solution)/shard_map/ppermute | solution.py:138
  67.9 1.8 %collective-permute-done = bf16[32,44,200]{2,0,1:T(8,128)(2,1)S(1)} collective-permute-done((bf16[32,44,200]{2,0,1:T(8,128)(2,1)S(1)}, bf16[32,44,200]{2,0,1:T(8,128)(2,1)S(1)}, u32[]{:S(2)}, u32[]{:S(2)}) %collective-permute-start) | collective-permute-done | bytes 563232 | tf_op jit(solution)/shard_map/ppermute | solution.py:138
  69.7 0.4 copy.4.other_ref
  70.1 3.8 %contract.1 = f32[16,64,128]{2,1,0:T(8,128)S(1)} custom-call(s32[1]{0:T(128)} %bitcast.ring_ref, bf16[32,44,200]{2,1,0:T(8,128)(2,1)S(1)} %all-gather.1.mine_ref, bf16[32,44,200]{2,1,0:T(8,128)(2,1)S(1)} %copy.4.other_ref, bf16[2816,640]{1,0:T(8,128)(2,1)} %integrals_hbm.1), custom_call_target="tpu_custom_call" | custom-call | flops 720896000 | bytes 4730880 | tf_op jit(solution)/shard_map/contract/pallas_call | solution.py:59
  73.9 15.7 %all_to_all.10.terms_ref = f32[16,64,128]{2,1,0:T(8,128)S(1)} all-to-all(f32[16,64,128]{2,1,0:T(8,128)S(1)} %contract.1), channel_id=1, replica_groups={{960,896,832,768,704,640,576,512,448,384,320,256,192,128,64,0},{961,897..., dimensions={0} | all-to-all | bytes 1048576 | tf_op jit(solution)/shard_map/all_to_all | solution.py:144
  89.6 13.3 %all_to_all.11 = bf16[16,64,128]{2,1,0:T(8,128)(2,1)S(1)} all-to-all(bf16[16,64,128]{2,1,0:T(8,128)(2,1)S(1)} %totals.1), channel_id=1, replica_groups=mesh['row'=16,'depth'=64] {'row'}, dimensions={0} | all-to-all | bytes 524288 | tf_op jit(solution)/shard_map/all_to_all | solution.py:145
  102.9 0.7 ordered.1
  (1 shorter events, 0.0 us)
Async XLA Ops:
  65.6 4.1 %collective-permute-start = (bf16[32,44,200]{2,0,1:T(8,128)(2,1)S(1)}, bf16[32,44,200]{2,0,1:T(8,128)(2,1)S(1)}, u32[]{:S(2)}, u32[]{:S(2)}) collective-permute-start(bf16[32,44,200]{2,0,1:T(8,128)(2,1)S(1)} %copy.3), channel_id=1, source_target_pairs={{0,1},{1,0},{2,3},{3,2},{4,5},{5,4},{6,7},{7,6},{8,9},{9,8},{10,11... | collective-permute-start | bytes 1689608 | tf_op jit(solution)/shard_map/ppermute | solution.py:138

commit v8 on v7

--- a/solution.py
+++ b/solution.py
@@ -23,8 +23,7 @@
         while done < values.shape[0]:
             owner, at = divmod(line + done, share)
             size = min(share - at, values.shape[0] - done)
-            slot = members - 1 - owner
-            out_ref[slot, at : at + size, :] = values[done : done + size]
+            out_ref[owner, at : at + size, :] = values[done : done + size]
             done += size
 
     even = ring_ref[0] == 0
@@ -142,7 +141,9 @@
         share = -(-ij * ab // (LANES * rows * 16)) * 16
         partial = contract(ring, mine, other, integrals, rows, share)
         terms = lax.all_to_all(partial, "row", 0, 0, axis_index_groups=turned)
-        whole = lax.all_to_all(totals(terms), "row", 0, 0)
+        whole = lax.all_to_all(
+            totals(terms), "row", 0, 0, axis_index_groups=turned
+        )
         return ordered(whole.reshape(rows * share, LANES), ij, ab).T
 
     placed = (P("row", "depth"), P(("row", "depth"), None))

time: 104 us -> 103 us (level)
  blocking collectives: 94.4 us -> 93.2 us
    all_to_all x1, blocking collectives: 13.3 us -> 12.1 us  [shards(): whole = lax.all_to_all(totals(terms), 'row', 0, 0, axis_index_groups=turned)]
where the time goes in v8:
time: 103 us; the launch traced here: 102 us
  blocking collectives  93.2 us (90%)
  Pallas kernels  4.56 us (4%)
  starting transfers between devices  2.3 us (2%)
  waiting for transfers between devices  1.78 us (2%)
    all_gather x1, blocking collectives, shards(): mine = lax.all_gather(amplitudes, 'depth', axis_index_groups=rings)  65.4 us
    all_to_all x1, blocking collectives, shards(): terms = lax.all_to_all(partial, 'row', 0, 0, axis_index_groups=turned)  15.7 us
    all_to_all x1, blocking collectives, shards(): whole = lax.all_to_all(totals(terms), 'row', 0, 0, axis_index_groups=turned)  12.1 us
    pallas_call x1, Pallas kernels, contract(): pl.pallas_call(contract_kernel, out_shape=jax.ShapeDtypeStruct((rows, sha...  3.78 us
    ppermute x1, starting transfers between devices, shards(): other = lax.ppermute(mine, 'depth', swap)  2.3 us
  transfers between devices with their start and end apart: 1, of which 1 were waited for; matrix products, arithmetic and copies ran while one was open for 0% of the time, Pallas kernels for 0%

profile of v8, /device:TPU:8, one launch (start us, length us, event | category | flops | bytes accessed | tf_op | source)
XLA Modules:
  0.0 102.5 jit_solution(11522931520066725615)
XLA Ops:
  0.0 65.4 %all-gather.1.mine_ref = bf16[32,44,200]{2,1,0:T(8,128)(2,1)S(1)} all-gather(bf16[1,44,200]{2,1,0:T(8,128)(2,1)} %bitcast.5), channel_id=2, replica_groups={{0,3,4,7,8,11,12,15,16,19,20,23,24,27,28,31,32,35,36,39,40,43,44,47,48,..., dimensions={0}, use_global_device_ids=true | all-gather | bytes 580800 | tf_op jit(solution)/shard_map/all_gather | solution.py:136
  65.4 0.2 copy.3
  65.6 2.3 %collective-permute-start = (bf16[32,44,200]{2,0,1:T(8,128)(2,1)S(1)}, bf16[32,44,200]{2,0,1:T(8,128)(2,1)S(1)}, u32[]{:S(2)}, u32[]{:S(2)}) collective-permute-start(bf16[32,44,200]{2,0,1:T(8,128)(2,1)S(1)} %copy.3), channel_id=1, source_target_pairs={{0,1},{1,0},{2,3},{3,2},{4,5},{5,4},{6,7},{7,6},{8,9},{9,8},{10,11... | collective-permute-start | bytes 1689608 | tf_op jit(solution)/shard_map/ppermute | solution.py:137
  67.9 1.8 %collective-permute-done = bf16[32,44,200]{2,0,1:T(8,128)(2,1)S(1)} collective-permute-done((bf16[32,44,200]{2,0,1:T(8,128)(2,1)S(1)}, bf16[32,44,200]{2,0,1:T(8,128)(2,1)S(1)}, u32[]{:S(2)}, u32[]{:S(2)}) %collective-permute-start) | collective-permute-done | bytes 563232 | tf_op jit(solution)/shard_map/ppermute | solution.py:137
  69.7 0.4 copy.4.other_ref
  70.1 3.8 %contract.1 = f32[16,64,128]{2,1,0:T(8,128)S(1)} custom-call(s32[1]{0:T(128)} %bitcast.ring_ref, bf16[32,44,200]{2,1,0:T(8,128)(2,1)S(1)} %all-gather.1.mine_ref, bf16[32,44,200]{2,1,0:T(8,128)(2,1)S(1)} %copy.4.other_ref, bf16[2816,640]{1,0:T(8,128)(2,1)} %integrals_hbm.1), custom_call_target="tpu_custom_call" | custom-call | flops 720896000 | bytes 4730880 | tf_op jit(solution)/shard_map/contract/pallas_call | solution.py:58
  73.9 15.7 %all_to_all.10.terms_ref = f32[16,64,128]{2,1,0:T(8,128)S(1)} all-to-all(f32[16,64,128]{2,1,0:T(8,128)S(1)} %contract.1), channel_id=1, replica_groups={{960,896,832,768,704,640,576,512,448,384,320,256,192,128,64,0},{961,897..., dimensions={0} | all-to-all | bytes 1048576 | tf_op jit(solution)/shard_map/all_to_all | solution.py:143
  89.6 12.1 %all_to_all.11 = bf16[16,64,128]{2,1,0:T(8,128)(2,1)S(1)} all-to-all(bf16[16,64,128]{2,1,0:T(8,128)(2,1)S(1)} %totals.1), channel_id=1, replica_groups={{960,896,832,768,704,640,576,512,448,384,320,256,192,128,64,0},{961,897..., dimensions={0} | all-to-all | bytes 524288 | tf_op jit(solution)/shard_map/all_to_all | solution.py:144
  101.7 0.7 ordered.1
  (1 shorter events, 0.0 us)
Async XLA Ops:
  65.6 4.1 %collective-permute-start = (bf16[32,44,200]{2,0,1:T(8,128)(2,1)S(1)}, bf16[32,44,200]{2,0,1:T(8,128)(2,1)S(1)}, u32[]{:S(2)}, u32[]{:S(2)}) collective-permute-start(bf16[32,44,200]{2,0,1:T(8,128)(2,1)S(1)} %copy.3), channel_id=1, source_target_pairs={{0,1},{1,0},{2,3},{3,2},{4,5},{5,4},{6,7},{7,6},{8,9},{9,8},{10,11... | collective-permute-start | bytes 1689608 | tf_op jit(solution)/shard_map/ppermute | solution.py:137
